TPU v7x, 256 devices: a whole 4x4x8 slice. The times are simulated.
256 devices in a mesh: users: 16 (over x, y), items: 16 (over z, core).
Axes of the slice: x: 4, y: 4, z: 8, core: 2. Of those that a mesh axis runs over, the one named last changes fastest.
Arguments:
- ratings: bfloat16 [32768, 8192], P('users', 'items')
- observed: int32 [32768, 8192], P('users', 'items'), may hold values 0 or 1
- pool_profiles: bfloat16 [24576, 8192], P('users', 'items')
- neighbours: int32 [64, 2], P('users'), may hold values from 0 to 63, as said below
- test_matrix: bfloat16 [32768, 256], P('users'), may hold values from -6 to 6
Outputs:
- imputed: bfloat16 [32768, 8192], P('users', 'items')
- sketch: float32 [256, 8192], P('users', 'items')
Inputs may be any that keep to these rules, and one draw needn't show every extreme that they name: `neighbours`: the 2 blocks of one query block are held by different indices of users; all query blocks of one index of users together name at most 1 block held by any one index of users, and exactly 1 from some.
All inputs are finite; a program needn't handle non-finite values. No bound on the sum of `observed` on one device may be relied on, other than what follows from the above.
Results may differ from a plain program's by a relative error of at most 0.0041.
Values may be sent and summed in bfloat16 or wider, within the bound.
A program may use at most 128 MiB of HBM per device.

v0:
```python
import math

import jax
import jax.numpy as jnp
from jax import lax
from jax.sharding import PartitionSpec as P

NB = 2
PBLK = 384


def body(ratings, observed, pool_profiles, neighbours, test_matrix):
    user_count = lax.axis_size("users")
    item_count = lax.axis_size("items")
    query_rows, item_cols = ratings.shape
    item_total = item_cols * item_count
    pool_rows = pool_profiles.shape[0]
    blocks_here = pool_rows // PBLK
    query_blocks = neighbours.shape[0]
    block_rows = query_rows // query_blocks
    near_total = NB * PBLK
    seen_float = observed.astype(jnp.float32)
    rated = ratings.astype(jnp.float32)
    pool_float = pool_profiles.astype(jnp.float32)
    local_sum = jnp.sum(seen_float * rated, axis=1)
    local_count = jnp.sum(seen_float, axis=1)
    query_sum, query_count, pool_sum = lax.psum(
        (local_sum, local_count, jnp.sum(pool_float, axis=1)), "items"
    )
    pool_mean = pool_sum / item_total
    squares_sum = lax.psum(jnp.sum(jnp.square(pool_float - pool_mean[:, None]), axis=1), "items")
    pool_var = squares_sum / item_total
    query_mean = query_sum / (query_count + 1.0)
    centered = (seen_float * (rated - query_mean[:, None])).astype(jnp.bfloat16)
    mean_half = pool_mean.astype(jnp.bfloat16)
    scale_half = lax.rsqrt(pool_var + 1e-05).astype(jnp.bfloat16)
    request_ids = neighbours.reshape(-1)
    request_total = request_ids.shape[0]
    capacity = max(1, request_total // user_count)
    owners = request_ids // blocks_here
    local_ids = request_ids % blocks_here
    positions = jnp.arange(request_total, dtype=jnp.int32)
    same_owner = owners[:, None] == owners[None, :]
    earlier = positions[:, None] > positions[None, :]
    ranked = jnp.sum((same_owner & earlier).astype(jnp.int32), axis=1)
    slots = owners * capacity + ranked
    onehot = (slots[:, None] == jnp.arange(user_count * capacity, dtype=jnp.int32)[None, :]).astype(
        jnp.int32
    )
    ask_table = jnp.sum(onehot * local_ids[:, None], axis=0).reshape(user_count, capacity)
    asked = lax.all_to_all(ask_table, "users", split_axis=0, concat_axis=0, tiled=True)
    pool_blocks = pool_profiles.reshape(blocks_here, PBLK, item_cols)
    block_stats = jnp.stack(
        [mean_half.reshape(blocks_here, PBLK), scale_half.reshape(blocks_here, PBLK)], axis=1
    )
    outgoing = jnp.take(pool_blocks, asked, axis=0)
    out_stats = jnp.take(block_stats, asked, axis=0)
    arrived, arrived_stats = (
        lax.all_to_all(outgoing, "users", split_axis=0, concat_axis=0, tiled=True),
        lax.all_to_all(out_stats, "users", split_axis=0, concat_axis=0, tiled=True),
    )
    fetched = jnp.take(arrived.reshape(user_count * capacity, PBLK, item_cols), slots, axis=0)
    fetched = fetched.reshape(query_blocks, near_total, item_cols)
    fetch_stats = jnp.take(arrived_stats.reshape(user_count * capacity, 2, PBLK), slots, axis=0)
    fetch_stats = fetch_stats.reshape(query_blocks, NB, 2, PBLK)
    near_mean = fetch_stats[:, :, 0, :].reshape(query_blocks, near_total)
    near_scale = fetch_stats[:, :, 1, :].reshape(query_blocks, near_total).astype(jnp.float32)
    query_view = centered.reshape(query_blocks, block_rows, item_cols)
    raw_dots = jnp.einsum("bqi,bni->bqn", query_view, fetched, preferred_element_type=jnp.float32)
    summed = lax.psum(raw_dots, "items")
    similar = summed * near_scale[:, None, :]
    weights = (
        similar * lax.rsqrt(jnp.sum(similar * similar, axis=2, keepdims=True) + 1e-06)
    ).astype(jnp.bfloat16)
    shift_term = jnp.einsum("bqn,bni->bqi", weights, fetched, preferred_element_type=jnp.float32)
    mean_term = jnp.einsum("bqn,bn->bq", weights, near_mean, preferred_element_type=jnp.float32)
    shift_term = (shift_term - mean_term[:, :, None]).reshape(query_rows, item_cols)
    filled = query_mean[:, None] + shift_term
    imputed = jnp.where(observed > 0, rated, filled).astype(jnp.bfloat16)
    partial_value = lax.psum_scatter(
        lax.dot_general(
            test_matrix, imputed, (((0,), (0,)), ((), ())), preferred_element_type=jnp.float32
        ),
        "users",
        scatter_dimension=0,
        tiled=True,
    )
    sketch = partial_value * (1.0 / math.sqrt(query_rows * user_count))
    return (imputed, sketch)


def solution(mesh):
    in_specs = (
        P("users", "items"),
        P("users", "items"),
        P("users", "items"),
        P("users", None),
        P("users", None),
    )
    out_specs = (P("users", "items"), P("users", "items"))
    return jax.shard_map(body, mesh=mesh, in_specs=in_specs, out_specs=out_specs, check_vma=False)
```

profile of v0, /device:TPU:1, one launch (start us, length us, event | category | flops | bytes accessed | tf_op | source)
XLA Modules:
  0.0 378.1 jit_solution(8654162319460735590)
XLA Ops:
  7.2 0.0 copy-start
  7.2 0.9 copy.59
  8.0 0.1 reshape.257
  8.1 0.2 convert_reduce_fusion.2
  8.3 0.1 select_reduce_fusion
  8.4 0.1 copy.65
  8.5 13.8 %all_to_all.19 = s32[16,1,1]{2,1,0:T(1,128)S(1)} all-to-all(s32[16,1,1]{2,1,0:T(1,128)S(1)} %copy.65), channel_id=1, replica_groups=mesh['users'=16,'items'=16] {'users'}, dimensions={0} | all-to-all | bytes 128 | tf_op jit(solution)/shard_map/all_to_all | solution.py:51
  22.3 0.4 and_reduce_fusion
  22.7 0.4 reduce.1
  23.1 5.0 %gather_fusion = bf16[16,384,512]{2,1,0:T(8,128)(2,1)} fusion(bf16[4,384,512]{2,1,0:T(8,128)(2,1)} %bitcast.47, s32[1024]{0:T(1024)S(1)} %pad_clamp_fusion.1), kind=kCustom, calls=%fused_computation | custom fusion | bytes 12582976 | tf_op jit(solution)/shard_map/jit(_take)/gather | solution.py:56
  28.1 6.1 %bitcast_select_fusion = bf16[16,1,384,512]{3,2,1,0:T(8,128)(2,1)} fusion(bf16[16,384,512]{2,1,0:T(8,128)(2,1)} %gather_fusion, pred[16]{0:T(512)(128)(4,1)S(1)} %get-tuple-element.19), kind=kLoop, calls=%fused_computation.4 | loop fusion | flops 3145728 | bytes 12582928 | tf_op jit(solution)/shard_map/jit(_take)/select_n | solution.py:56
  34.2 0.0 copy-start.2
  34.2 4.8 %all-to-all-start.1 = ((bf16[16,1,384,512]{3,2,1,0:T(8,128)(2,1)}), bf16[16,1,384,512]{3,2,1,0:T(8,128)(2,1)}, u32[]{:S(2)}, u32[]{:S(2)}) async-start(bf16[16,1,384,512]{3,2,1,0:T(8,128)(2,1)} %bitcast_select_fusion), calls=%async_computation.1 | async-start | bytes 12582912 | tf_op jit(solution)/shard_map/all_to_all | solution.py:59
  39.0 0.0 all-reduce.3.cloned.1.call-start
  39.0 0.1 reshape.260
  39.1 0.1 reduce_sum.70
  39.2 0.1 copy.64
  39.3 0.0 copy-done.2
  39.3 0.3 convert_reduce_fusion.1
  39.6 29.7 %psum.38 = f32[1536]{0:T(1024)S(1)} all-reduce(f32[1536]{0:T(1024)S(1)} %convert_reduce_fusion.1), channel_id=1, replica_groups=mesh['users'=16,'items'=16] {'items'}, use_global_device_ids=true, to_apply=%region_8.9 | all-reduce | flops 1536 | bytes 12288 | tf_op jit(solution)/shard_map/psum | solution.py:27
  69.3 0.8 fusion.5
  70.1 0.0 copy-start.6
  70.1 4.0 %convert_reduce_fusion = (f32[2048]{0:T(1024)S(1)}, f32[2048]{0:T(1024)S(1)}) fusion(s32[2048,512]{1,0:T(8,128)} %param.6, bf16[2048,512]{1,0:T(8,128)(2,1)} %param.5), kind=kLoop, calls=%fused_computation.15 | loop fusion | flops 5238784 | bytes 6307840 | tf_op jit(solution)/shard_map/reduce_sum | solution.py:26
  74.2 46.5 %all-reduce = (f32[1536]{0:T(1024)S(1)}, f32[2048]{0:T(1024)S(1)}, f32[2048]{0:T(1024)S(1)}) all-reduce(f32[1536]{0:T(1024)S(1)} %fusion.5, f32[2048]{0:T(1024)S(1)} %get-tuple-element.15, f32[2048]{0:T(1024)S(1)} %get-tuple-element.14), channel_id=1, replica_groups=mesh['users'=16,'items'=16] {'items'}, use_global_device_ids=true, to_apply=%region_10.11 | all-reduce | flops 5632 | bytes 45056 | tf_op jit(solution)/shard_map/psum | solution.py:31
  120.7 0.0 copy-done.6
  120.7 4.2 %fusion.2 = bf16[2048,512]{1,0:T(8,128)(2,1)} fusion(bf16[2048,512]{1,0:T(8,128)(2,1)S(1)} %copy-done.6, s32[2048,512]{1,0:T(8,128)} %param.6, f32[2048]{0:T(1024)S(1)} %add_divide_fusion), kind=kLoop, calls=%fused_computation.12 | loop fusion | flops 5242880 | bytes 8396800 | tf_op jit(solution)/shard_map/convert_element_type | solution.py:34
  124.9 8.3 %all-to-all-done.1 = bf16[16,1,384,512]{3,2,1,0:T(8,128)(2,1)} async-done(((bf16[16,1,384,512]{3,2,1,0:T(8,128)(2,1)}), bf16[16,1,384,512]{3,2,1,0:T(8,128)(2,1)}, u32[]{:S(2)}, u32[]{:S(2)}) %all-to-all-start.1) | async-done | bytes 6291488 | tf_op jit(solution)/shard_map/all_to_all | solution.py:59
  133.3 5.2 %gather_fusion.1 = bf16[8,384,512]{2,1,0:T(8,128)(2,1)} fusion(bf16[16,384,512]{2,1,0:T(8,128)(2,1)} %bitcast.5, s32[1024]{0:T(1024)S(1)} %pad_clamp_fusion), kind=kCustom, calls=%fused_computation.1 | custom fusion | bytes 6291488 | tf_op jit(solution)/shard_map/jit(_take)/gather | solution.py:62
  138.5 0.0 copy-start.7
  138.5 0.1 broadcast_in_dim.57
  138.6 2.3 bitcast_select_fusion.1
  140.9 0.0 copy-start.3
  140.9 1.7 copy-done.3
  142.6 0.0 copy-done.7
  142.6 4.5 %fusion.14 = f32[4,512,768]{2,1,0:T(8,128)} fusion(bf16[4,512,512]{2,1,0:T(8,128)(2,1)S(1)} %bitcast.48, bf16[4,768,512]{2,1,0:T(8,128)(2,1)S(1)} %bitcast_select_fusion.1), kind=kOutput, calls=%fused_computation.67 | convolution fusion | flops 1610612736 | bytes 11534336 | tf_op jit(solution)/shard_map/bqi,bni->bqn/dot_general | solution.py:69
  147.0 0.0 all-reduce.3.cloned.1.call-update
  147.1 0.0 reduce-scatter.4.cloned.1.call-start
  147.2 0.6 gather_fusion.2
  147.8 0.1 fusion.7
  147.9 13.5 %all_to_all.20 = bf16[16,1,2,384]{3,2,1,0:T(2,128)(2,1)S(1)} all-to-all(bf16[16,1,2,384]{3,2,1,0:T(2,128)(2,1)S(1)} %fusion.7), channel_id=1, replica_groups=mesh['users'=16,'items'=16] {'users'}, dimensions={0} | all-to-all | bytes 49152 | tf_op jit(solution)/shard_map/all_to_all | solution.py:60
  161.4 0.6 gather_fusion.3
  162.0 0.1 broadcast_select_fusion.1
  162.2 119.1 %all-reduce.3.cloned.1.call-done = f32[4,512,768]{2,1,0:T(8,128)} async-done(((f32[4,512,768]{2,1,0:T(8,128)}), f32[4,512,768]{2,1,0:T(8,128)}) %all-reduce.3.cloned.1.call-update) | async-done | bytes 6291472 | tf_op jit(solution)/shard_map/psum | solution.py:70
  281.3 0.0 copy-start.1
  281.3 3.6 multiply_reduce_fusion
  284.9 0.0 copy-start.4
  284.9 0.9 copy-done.1
  285.9 1.0 fusion.6
  286.9 0.2 copy-done.4
  287.1 0.0 copy-start.5
  287.1 2.1 broadcast_subtract_fusion
  289.2 0.1 copy-done.5
  289.2 0.7 fusion.3
  290.0 0.0 copy-start.8
  290.0 1.3 copy-done.8
  291.3 0.0 copy-done
  291.3 0.7 convolution_bitcast_fusion
  292.1 1.0 copy.74
  293.0 0.0 reduce-scatter.4.cloned.1.call-update
  293.1 76.6 %reduce-scatter.4.cloned.1.call-done = f32[16,512]{1,0:T(8,128)} async-done(((f32[256,512]{1,0:T(8,128)}), f32[16,512]{1,0:T(8,128)}) %reduce-scatter.4.cloned.1.call-update) | async-done | bytes 32784
  369.6 0.9 copy.75
  370.5 0.7 copy.71
  (18 shorter events, 0.2 us)
Async XLA Ops:
  7.2 284.1 %copy-start = (bf16[2048,256]{1,0:T(8,128)(2,1)S(1)}, bf16[2048,256]{1,0:T(8,128)(2,1)}, u32[]{:S(2)}) copy-start(bf16[2048,256]{1,0:T(8,128)(2,1)} %param.9) | copy-start | bytes 3145732
  34.2 5.1 %copy-start.2 = (bf16[1536,512]{1,0:T(8,128)(2,1)S(1)}, bf16[1536,512]{1,0:T(8,128)(2,1)}, u32[]{:S(2)}) copy-start(bf16[1536,512]{1,0:T(8,128)(2,1)} %param.7) | copy-start | bytes 4718596
  34.2 99.1 %all-to-all-start.1 = ((bf16[16,1,384,512]{3,2,1,0:T(8,128)(2,1)}), bf16[16,1,384,512]{3,2,1,0:T(8,128)(2,1)}, u32[]{:S(2)}, u32[]{:S(2)}) async-start(bf16[16,1,384,512]{3,2,1,0:T(8,128)(2,1)} %bitcast_select_fusion), calls=%async_computation.1 | async-start | bytes 12582912 | tf_op jit(solution)/shard_map/all_to_all | solution.py:59
  39.0 242.3 %all-reduce.3.cloned.1.call-start = ((), (), s32[]{:S(2)}) async-start(), calls=%async_computation.4 | async-start | bytes 12582912 | tf_op jit(solution)/shard_map/psum | solution.py:70
  70.1 50.6 %copy-start.6 = (bf16[2048,512]{1,0:T(8,128)(2,1)S(1)}, bf16[2048,512]{1,0:T(8,128)(2,1)}, u32[]{:S(2)}) copy-start(bf16[2048,512]{1,0:T(8,128)(2,1)} %param.5) | copy-start | bytes 6291460
  138.5 4.1 %copy-start.7 = (bf16[2048,512]{1,0:T(8,128)(2,1)S(1)}, bf16[2048,512]{1,0:T(8,128)(2,1)}, u32[]{:S(2)}) copy-start(bf16[2048,512]{1,0:T(8,128)(2,1)} %fusion.2) | copy-start | bytes 6291460
  140.9 1.7 copy-start.3
  147.1 222.6 %reduce-scatter.4.cloned.1.call-start = ((), (), s32[]{:S(2)}) async-start(), calls=%async_computation.5 | async-start | bytes 557056
  281.3 4.6 %copy-start.1 = (f32[4,512,768]{2,1,0:T(8,128)S(1)}, f32[4,512,768]{2,1,0:T(8,128)}, u32[]{:S(2)}) copy-start(f32[4,512,768]{2,1,0:T(8,128)} %all-reduce.3.cloned.1.call-done) | copy-start | bytes 18874372
  284.9 2.1 copy-start.4
  287.1 2.2 copy-start.5
  290.0 1.3 copy-start.8
Sparse Core Ops, SparseCore 0:
  147.2 134.0 all-reduce.2
  293.2 76.3 reduce-scatter.3
where the time goes:
time: 379 us; the launch traced here: 378 us
  waiting for transfers between devices  204 us (54%)
  blocking collectives  104 us (27%)
  other arithmetic  23.5 us (6%)
  local copies, waits for them, and re-layouts  19.6 us (5%)
  between operations  14.3 us (4%)
  matrix products  8.32 us (2%)
  starting transfers between devices  4.84 us (1%)
    psum x1, waiting for transfers between devices, body(): summed = lax.psum(raw_dots, 'items')  119 us
    unnamed x3, waiting for transfers between devices  76.6 us
    psum x1, blocking collectives, body(): lax.psum(jnp.sum(jnp.square(pool_float - pool_mean[:, None]), axis=1), 'i...  46.5 us
    psum x1, blocking collectives, body(): lax.psum((local_sum, local_count, jnp.sum(pool_float, axis=1)), 'items')  29.7 us
    all_to_all x1, blocking collectives, body(): lax.all_to_all(ask_table, 'users', split_axis=0, concat_axis=0, tiled=True)  13.8 us
    all_to_all x1, blocking collectives, body(): lax.all_to_all(out_stats, 'users', split_axis=0, concat_axis=0, tiled=True)  13.5 us
    all_to_all x1, waiting for transfers between devices, body(): lax.all_to_all(outgoing, 'users', split_axis=0, concat_axis=0, tiled=True)  8.35 us
    unnamed x23, local copies, waits for them, and re-layouts  7.64 us
  transfers between devices with their start and end apart: 3, of which 3 were waited for; matrix products, arithmetic and copies ran while one was open for 3% of the time, Pallas kernels for 0%

commit v1 on v0

v1 whole, which is shorter than its diff:
```python
import functools
import math

import jax
import jax.numpy as jnp
from jax import lax
from jax.experimental import pallas as pl
from jax.experimental.pallas import tpu as pltpu
from jax.sharding import PartitionSpec as P

MESH = pl.DeviceIdType.MESH
BF16 = jnp.bfloat16
F32 = jnp.float32

SIDE = 4
USERS = SIDE * SIDE
CHIPS = 8
PLUS = CHIPS // 2
MINUS = CHIPS - 1 - PLUS
ITEM_DEVS = 2 * CHIPS
QB = 4
QBLK = 512
PB = 4
PBLK = 384
NB = 2
NEAR = NB * PBLK
REQ = QB * NB
COLS = 512
KS = 256
HALF = QBLK // 2
CHUNK = HALF // CHIPS
ROWS = QB * QBLK
PROWS = PB * PBLK
PR = PBLK // SIDE
PC = COLS // SIDE
ITEMS = COLS * ITEM_DEVS
LAG = 5

ORDER = [
    (2, 2), (3, 2), (2, 3), (1, 2), (2, 1), (0, 2), (2, 0), (3, 1),
    (1, 3), (3, 3), (1, 1), (0, 3), (3, 0), (0, 1), (1, 0),
]


def nt(a, b):
    return lax.dot_general(a, b, (((1,), (1,)), ((), ())), preferred_element_type=F32)


def row_sums(x):
    ones = jnp.ones((8, 128), F32)
    return lax.dot_general(
        ones, x, (((1,), (1,)), ((), ())), precision=lax.Precision.HIGHEST, preferred_element_type=F32
    )[0:1]


def fold(x):
    return (x[:, 0:128] + x[:, 128:256]) + (x[:, 256:384] + x[:, 384:512])


def kernel(
    rat, obs, pool, nbr, test, imp, sketch,
    rat_v, obs_v, pool_v, test_v, nb_v, nb_s, spread, send2, near, cent, qm,
    st_own, st_in, ms_own, ms_all, sib_out, sib_in, own,
    up_out, up_in, dn_out, dn_in, wts, imp_v, sk, sk_in,
    ld, nb_ss, nb_rs, s1_ss, s1_rs, s2_ss, s2_rs, st_ss, st_rs, ms_ss, ms_rs,
    sib_ss, sib_rs, up_ss, up_rs, dn_ss, dn_rs, au_ss, au_rs, ad_ss, ad_rs,
    ax_ss, ax_rs, sk_ss, sk_rs, out_s,
):
    u = lax.axis_index("users")
    it = lax.axis_index("items")
    ux, uy = u // SIDE, u % SIDE
    z, c = it // 2, it % 2
    sent = []

    def user_at(dx, dy):
        return ((ux + dx) % SIDE) * SIDE + (uy + dy) % SIDE

    def chip_at(dz):
        return (u, ((z + dz + CHIPS) % CHIPS) * 2 + c)

    sibling = (u, z * 2 + (1 - c))

    def send(src, dst, ss, rs, dev):
        copy = pltpu.make_async_remote_copy(
            src_ref=src, dst_ref=dst, send_sem=ss, recv_sem=rs, device_id=dev, device_id_type=MESH
        )
        copy.start()
        sent.append(copy)

    def arrived(dst, ss, rs):
        pltpu.make_async_remote_copy(
            src_ref=dst, dst_ref=dst, send_sem=ss, recv_sem=rs, device_id=sibling, device_id_type=MESH
        ).wait_recv()

    def flush():
        for copy in sent:
            copy.wait_send()
        sent.clear()

    loads = [
        pltpu.make_async_copy(pool, pool_v, ld.at[0]),
        pltpu.make_async_copy(rat, rat_v, ld.at[1]),
        pltpu.make_async_copy(obs, obs_v, ld.at[2]),
        pltpu.make_async_copy(test, test_v, ld.at[3]),
        pltpu.make_async_copy(nbr, nb_v.at[u], ld.at[4]),
        pltpu.make_async_copy(
            pool.at[:, pl.ds(ux * PR, PR), pl.ds(pl.multiple_of(uy * PC, PC), PC)],
            spread.at[pl.ds(u * PB, PB)],
            ld.at[5],
        ),
    ]
    for load in loads:
        load.start()

    barrier = pltpu.get_barrier_semaphore()
    for dx, dy in ORDER:
        pl.semaphore_signal(barrier, inc=1, device_id=(user_at(dx, dy), it), device_id_type=MESH)
    for k in range(1, ITEM_DEVS):
        pl.semaphore_signal(
            barrier, inc=1, device_id=(u, (it + k) % ITEM_DEVS), device_id_type=MESH
        )
    pl.semaphore_wait(barrier, USERS - 1 + ITEM_DEVS - 1)

    for o, (dx, dy) in enumerate(ORDER):
        t = user_at(dx, dy)
        send(nbr, nb_v.at[u], nb_ss.at[o], nb_rs.at[o], (t, it))
    for o, (dx, dy) in enumerate(ORDER):
        t = user_at(dx, dy)
        send(
            pool.at[:, pl.ds((t // SIDE) * PR, PR), pl.ds(pl.multiple_of((t % SIDE) * PC, PC), PC)],
            spread.at[pl.ds(u * PB, PB)],
            s1_ss.at[o], s1_rs.at[o], (t, it),
        )

    loads[0].wait()
    for b in range(PB):
        p = pool_v[b].astype(F32)
        part = fold(p)
        mean = jnp.sum(part, axis=1, keepdims=True) * (1.0 / COLS)
        dev = p - mean
        st_own[2:3, b * PBLK:(b + 1) * PBLK] = row_sums(part)
        st_own[3:4, b * PBLK:(b + 1) * PBLK] = row_sums(fold(dev * dev))
    st_own[2:4, PROWS:ROWS] = jnp.zeros((2, ROWS - PROWS), F32)
    loads[1].wait()
    loads[2].wait()
    ones = jnp.ones((8, COLS), BF16)
    for b in range(ROWS // 256):
        rows = slice(b * 256, (b + 1) * 256)
        seen = obs_v[rows].astype(F32)
        masked = (seen * rat_v[rows].astype(F32)).astype(BF16)
        st_own[0:1, rows] = nt(ones, masked)[0:1]
        st_own[1:2, rows] = nt(ones, seen.astype(BF16))[0:1]
    for k in range(1, ITEM_DEVS):
        send(
            st_own, st_in.at[it], st_ss.at[k - 1], st_rs.at[k - 1],
            (u, (it + k) % ITEM_DEVS),
        )
    st_in[it] = st_own[...]

    loads[4].wait()
    for o, (dx, dy) in enumerate(ORDER):
        arrived(nb_v.at[user_at(-dx + SIDE, -dy + SIDE)], nb_ss.at[o], nb_rs.at[o])
    lists = pltpu.make_async_copy(nb_v, nb_s, ld.at[6])
    lists.start()
    lists.wait()
    loads[5].wait()
    for o, (dx, dy) in enumerate(ORDER):
        src = user_at(-dx + SIDE, -dy + SIDE)
        arrived(spread.at[pl.ds(src * PB, PB)], s1_ss.at[o], s1_rs.at[o])

    def deliver(b):
        for o, (dx, dy) in enumerate(ORDER):
            t = user_at(dx, dy)
            for k in range(b * NB, (b + 1) * NB):
                send2[o, k] = spread[nb_s[t, 0, k]]
            send(
                send2.at[o, pl.ds(b * NB, NB)],
                near.at[pl.ds(b * NB, NB), pl.ds(ux * PR, PR), pl.ds(pl.multiple_of(uy * PC, PC), PC)],
                s2_ss.at[b, o], s2_rs.at[b, o], (t, it),
            )
        for k in range(b * NB, (b + 1) * NB):
            near[k, pl.ds(pl.multiple_of(ux * PR, PR), PR), pl.ds(pl.multiple_of(uy * PC, PC), PC)] = spread[
                nb_s[u, 0, k]
            ]

    def delivered(b):
        for o, (dx, dy) in enumerate(ORDER):
            src = user_at(-dx + SIDE, -dy + SIDE)
            arrived(
                near.at[
                    pl.ds(b * NB, NB),
                    pl.ds((src // SIDE) * PR, PR),
                    pl.ds(pl.multiple_of((src % SIDE) * PC, PC), PC),
                ],
                s2_ss.at[b, o], s2_rs.at[b, o],
            )

    deliver(0)
    deliver(1)

    for k in range(1, ITEM_DEVS):
        src = (it + ITEM_DEVS - k) % ITEM_DEVS
        arrived(st_in.at[src], st_ss.at[k - 1], st_rs.at[k - 1])
    sums = st_in[0]
    for k in range(1, ITEM_DEVS):
        sums = sums + st_in[k]
    pool_mean = sums[2:3, 0:PROWS] * (1.0 / ITEMS)
    squares = sums[3:4, 0:PROWS]
    for k in range(ITEM_DEVS):
        gap = st_in[k, 2:3, 0:PROWS] * (1.0 / COLS) - pool_mean
        squares = squares + COLS * (gap * gap)
    scale = lax.rsqrt(squares * (1.0 / ITEMS) + 1e-05)
    blank = jnp.zeros((2, 128), F32)
    for b in range(PB):
        tiles = []
        for v in (pool_mean, scale):
            for j in range(PBLK // 128):
                at = b * PBLK + j * 128
                tiles.append(v[0:1, at:at + 128])
        tile = jnp.concatenate(tiles + [blank], axis=0)
        ms_own[b // 2, (b % 2) * 8:(b % 2) * 8 + 8] = tile
    ms_all[pl.ds(u * (PB // 2), PB // 2)] = ms_own[...].astype(BF16)
    for o, (dx, dy) in enumerate(ORDER):
        mine = ms_all.at[pl.ds(u * (PB // 2), PB // 2)]
        send(mine, mine, ms_ss.at[o], ms_rs.at[o], (user_at(dx, dy), it))
    deliver(2)
    deliver(3)

    def spread_mean(k, carry):
        at = pl.multiple_of(k * 128, 128)
        row = st_own[0:1, pl.ds(at, 128)]
        wide = jnp.broadcast_to(row, (128, 128)).T
        qm[pl.ds(at, 128)] = wide
        mean = jnp.concatenate([wide] * (COLS // 128), axis=1)
        seen = obs_v[pl.ds(at, 128)].astype(F32)
        cent[pl.ds(at, 128)] = (seen * (rat_v[pl.ds(at, 128)].astype(F32) - mean)).astype(BF16)
        return carry

    for copy in sent[2 * (USERS - 1):2 * (USERS - 1) + ITEM_DEVS - 1]:
        copy.wait_send()
    del sent[2 * (USERS - 1):2 * (USERS - 1) + ITEM_DEVS - 1]
    st_own[0:1] = sums[0:1] / (sums[1:2] + 1.0)
    lax.fori_loop(0, ROWS // 128, spread_mean, 0)
    for o, (dx, dy) in enumerate(ORDER):
        src = user_at(-dx + SIDE, -dy + SIDE)
        arrived(ms_all.at[pl.ds(src * (PB // 2), PB // 2)], ms_ss.at[o], ms_rs.at[o])
    loads[3].wait()

    up, down = chip_at(1), chip_at(-1)
    mine_at = c * HALF

    def stats_of(b):
        means, scales = [], []
        for k in range(b * NB, (b + 1) * NB):
            n = nb_s[u, 0, k]
            pair = ms_all[n // 2].astype(F32)
            tile = jnp.where(n % 2 == 0, pair[0:8], pair[8:16])
            means += [tile[j:j + 1] for j in range(3)]
            scales += [tile[j:j + 1] for j in range(3, 6)]
        return jnp.concatenate(means, axis=1), jnp.concatenate(scales, axis=1)

    def fill(b, at):
        w = wts[b, pl.ds(at, HALF)]
        pools = near[b * NB:(b + 1) * NB].reshape(NEAR, COLS)
        mean_row, _ = stats_of(b)
        mean_mat = jnp.broadcast_to(mean_row, (128, NEAR)).astype(BF16)
        shift = jnp.dot(w, pools, preferred_element_type=F32)
        rows = pl.ds(b * QBLK + at, HALF)
        base = qm[rows] - nt(w, mean_mat)
        filled = jnp.concatenate([base] * (COLS // 128), axis=1) + shift
        imp_v[rows] = jnp.where(obs_v[rows] > 0, rat_v[rows].astype(F32), filled).astype(BF16)

    def block(b):
        yield
        delivered(b)
        pools = near[b * NB:(b + 1) * NB].reshape(NEAR, COLS)
        theirs = pl.multiple_of(b * QBLK + (1 - c) * HALF, HALF)
        sib_out[b] = nt(cent[pl.ds(theirs, HALF)], pools).astype(BF16)
        send(sib_out.at[b], sib_in.at[b], sib_ss.at[b], sib_rs.at[b], sibling)
        mine = pl.multiple_of(b * QBLK + mine_at, HALF)
        own[b] = nt(cent[pl.ds(mine, HALF)], pools)
        yield
        arrived(sib_in.at[b], sib_ss.at[b], sib_rs.at[b])
        own[b] = own[b] + sib_in[b].astype(F32)

        def chunk(d):
            return own[b, pl.ds(pl.multiple_of(((z + d + CHIPS) % CHIPS) * CHUNK, CHUNK), CHUNK)]

        for s in range(PLUS):
            value = chunk(PLUS - s)
            if s > 0:
                arrived(up_in.at[b, s - 1], up_ss.at[b, s - 1], up_rs.at[b, s - 1])
                value = value + up_in[b, s - 1].astype(F32)
            up_out[b, s] = value.astype(BF16)
            send(up_out.at[b, s], up_in.at[b, s], up_ss.at[b, s], up_rs.at[b, s], up)
            if s < MINUS:
                value = chunk(s - MINUS)
                if s > 0:
                    arrived(dn_in.at[b, s - 1], dn_ss.at[b, s - 1], dn_rs.at[b, s - 1])
                    value = value + dn_in[b, s - 1].astype(F32)
                dn_out[b, s] = value.astype(BF16)
                send(dn_out.at[b, s], dn_in.at[b, s], dn_ss.at[b, s], dn_rs.at[b, s], down)
            yield
        s = PLUS - 1
        arrived(up_in.at[b, s], up_ss.at[b, s], up_rs.at[b, s])
        s = MINUS - 1
        arrived(dn_in.at[b, s], dn_ss.at[b, s], dn_rs.at[b, s])
        total = chunk(0) + (up_in[b, PLUS - 1].astype(F32) + dn_in[b, MINUS - 1].astype(F32))
        _, scale_row = stats_of(b)
        similar = total * scale_row
        norm = lax.rsqrt(jnp.sum(similar * similar, axis=1, keepdims=True) + 1e-06)

        def place(d, core):
            at = pl.multiple_of(core * HALF + ((z + d + CHIPS) % CHIPS) * CHUNK, CHUNK)
            return wts.at[b, pl.ds(at, CHUNK)]

        at = pl.multiple_of(mine_at + z * CHUNK, CHUNK)
        wts[b, pl.ds(at, CHUNK)] = (similar * norm).astype(BF16)

        def share(d, j):
            send(place(d, c), place(d, c), ax_ss.at[b, j], ax_rs.at[b, j], sibling)

        for s in range(PLUS):
            if s > 0:
                arrived(place(-s, c), au_ss.at[b, s - 1], au_rs.at[b, s - 1])
            send(place(-s, c), place(-s, c), au_ss.at[b, s], au_rs.at[b, s], up)
            if s < MINUS:
                if s > 0:
                    arrived(place(s, c), ad_ss.at[b, s - 1], ad_rs.at[b, s - 1])
                send(place(s, c), place(s, c), ad_ss.at[b, s], ad_rs.at[b, s], down)
                share(s, s)
            if s > 0:
                share(-s, MINUS + s)
            yield
        arrived(place(MINUS, c), ad_ss.at[b, MINUS - 1], ad_rs.at[b, MINUS - 1])
        share(MINUS, MINUS)
        arrived(place(-PLUS, c), au_ss.at[b, PLUS - 1], au_rs.at[b, PLUS - 1])
        share(-PLUS, MINUS + PLUS)
        fill(b, pl.multiple_of(mine_at, HALF))
        yield
        for d in range(MINUS + 1):
            arrived(place(d, 1 - c), ax_ss.at[b, d], ax_rs.at[b, d])
        for s in range(1, PLUS + 1):
            arrived(place(-s, 1 - c), ax_ss.at[b, MINUS + s], ax_rs.at[b, MINUS + s])
        fill(b, pl.multiple_of((1 - c) * HALF, HALF))
        rows = slice(b * QBLK, (b + 1) * QBLK)
        pltpu.make_async_copy(imp_v.at[rows], imp.at[rows], out_s.at[b]).start()
        part = lax.dot_general(
            test_v[rows], imp_v[rows], (((0,), (0,)), ((), ())), preferred_element_type=F32
        ).reshape(USERS, KS // USERS, COLS)
        sk[...] = part if b == 0 else sk[...] + part

    runs = [block(b) for b in range(QB)]
    live = list(range(QB))
    tick = 0
    while live:
        for b in list(live):
            if tick >= b * LAG and next(runs[b], "end") == "end":
                live.remove(b)
        tick += 1

    for o, (dx, dy) in enumerate(ORDER):
        t = user_at(dx, dy)
        send(sk.at[t], sk_in.at[u], sk_ss.at[o], sk_rs.at[o], (t, it))
    sk_in[u] = sk[u]
    for copy in sent[:-(USERS - 1)]:
        copy.wait_send()
    del sent[:-(USERS - 1)]
    for b in range(QB):
        rows = slice(b * QBLK, (b + 1) * QBLK)
        pltpu.make_async_copy(imp_v.at[rows], imp.at[rows], out_s.at[b]).wait()
    for o, (dx, dy) in enumerate(ORDER):
        arrived(sk_in.at[user_at(-dx + SIDE, -dy + SIDE)], sk_ss.at[o], sk_rs.at[o])
    total = sk_in[0]
    for k in range(1, USERS):
        total = total + sk_in[k]
    sketch[...] = total * (1.0 / math.sqrt(ROWS * USERS))
    flush()


def body(ratings, observed, pool_profiles, neighbours, test_matrix):
    lists = jnp.pad(neighbours.reshape(1, REQ), ((0, 7), (0, 128 - REQ)))
    pool = pool_profiles.reshape(PB, PBLK, COLS)
    dma = pltpu.SemaphoreType.DMA
    n = USERS - 1
    scratch = [
        pltpu.VMEM((ROWS, COLS), BF16),
        pltpu.VMEM((ROWS, COLS), jnp.int32),
        pltpu.VMEM((PB, PBLK, COLS), BF16),
        pltpu.VMEM((ROWS, KS), BF16),
        pltpu.VMEM((USERS, 8, 128), jnp.int32),
        pltpu.SMEM((USERS, 8, 128), jnp.int32),
        pltpu.VMEM((USERS * PB, PR, PC), BF16),
        pltpu.VMEM((n, REQ, PR, PC), BF16),
        pltpu.VMEM((REQ, PBLK, COLS), BF16),
        pltpu.VMEM((ROWS, COLS), BF16),
        pltpu.VMEM((ROWS, 128), F32),
        pltpu.VMEM((4, ROWS), F32),
        pltpu.VMEM((ITEM_DEVS, 4, ROWS), F32),
        pltpu.VMEM((PB // 2, 16, 128), F32),
        pltpu.VMEM((USERS * PB // 2, 16, 128), BF16),
        pltpu.VMEM((QB, HALF, NEAR), BF16),
        pltpu.VMEM((QB, HALF, NEAR), BF16),
        pltpu.VMEM((QB, HALF, NEAR), F32),
        pltpu.VMEM((QB, PLUS, CHUNK, NEAR), BF16),
        pltpu.VMEM((QB, PLUS, CHUNK, NEAR), BF16),
        pltpu.VMEM((QB, MINUS, CHUNK, NEAR), BF16),
        pltpu.VMEM((QB, MINUS, CHUNK, NEAR), BF16),
        pltpu.VMEM((QB, QBLK, NEAR), BF16),
        pltpu.VMEM((ROWS, COLS), BF16),
        pltpu.VMEM((USERS, KS // USERS, COLS), F32),
        pltpu.VMEM((USERS, KS // USERS, COLS), F32),
        dma((7,)),
    ]
    for shape in ((n,), (n,), (QB, n), (ITEM_DEVS - 1,), (n,), (QB,), (QB, PLUS), (QB, MINUS),
                  (QB, PLUS), (QB, MINUS), (QB, CHIPS), (n,)):
        scratch += [dma(shape), dma(shape)]
    scratch.append(dma((QB,)))
    hbm = pl.BlockSpec(memory_space=pl.ANY)
    vmem = pl.BlockSpec(memory_space=pltpu.VMEM)
    return pl.pallas_call(
        kernel,
        out_shape=(
            jax.ShapeDtypeStruct((ROWS, COLS), BF16),
            jax.ShapeDtypeStruct((KS // USERS, COLS), F32),
        ),
        in_specs=[hbm, hbm, hbm, vmem, hbm],
        out_specs=(hbm, vmem),
        scratch_shapes=scratch,
        compiler_params=pltpu.CompilerParams(
            collective_id=0, has_side_effects=True, vmem_limit_bytes=56 * 2**20
        ),
        name="impute_and_sketch",
    )(ratings, observed, pool, lists, test_matrix)


def solution(mesh):
    in_specs = (
        P("users", "items"),
        P("users", "items"),
        P("users", "items"),
        P("users", None),
        P("users", None),
    )
    out_specs = (P("users", "items"), P("users", "items"))
    return jax.shard_map(body, mesh=mesh, in_specs=in_specs, out_specs=out_specs, check_vma=False)
```

time: 379 us -> 161 us (0.42)
  waiting for transfers between devices: 204 us -> 0 us
  Pallas kernels: 0 us -> 155 us
  blocking collectives: 104 us -> 0 us
  other arithmetic: 23.5 us -> 0 us
  local copies, waits for them, and re-layouts: 19.6 us -> 5.12 us
  between operations: 14.3 us -> 0.65 us
  matrix products: 8.32 us -> 0 us
  starting transfers between devices: 4.84 us -> 0 us
    pallas_call x0 -> x1, Pallas kernels: none -> 155 us  [body(): pl.pallas_call(kernel, out_shape=(jax.ShapeDtypeStruct((ROWS, COLS), BF16...]
    psum x1 -> x0, waiting for transfers between devices: 119 us -> none  [body(): summed = lax.psum(raw_dots, 'items')]
    unnamed x3 -> x0, waiting for transfers between devices: 76.6 us -> none
    psum x2 -> x0, blocking collectives: 76.2 us -> none  [the longest x1 46.5 us: body(): lax.psum(jnp.sum(jnp.square(pool_float - pool_mean[:, None]), axis=1), 'i...]
    all_to_all x2 -> x0, blocking collectives: 27.3 us -> none  [the longest x1 13.8 us: body(): lax.all_to_all(ask_table, 'users', split_axis=0, concat_axis=0, tiled=True)]
    gather x4 -> x0, local copies, waits for them, and re-layouts: 11.4 us -> none  [the longest x1 5.23 us: body(): jnp.take(arrived.reshape(user_count * capacity, PBLK, item_cols), slots,...]
    reduce_sum x6 -> x0, other arithmetic: 9.02 us -> none  [the longest x1 4.04 us: body(): local_count = jnp.sum(seen_float, axis=1)]
    select_n x7 -> x0, other arithmetic: 9.01 us -> none  [the longest x2 6.49 us: body(): outgoing = jnp.take(pool_blocks, asked, axis=0)]
  transfers between devices with their start and end apart: 3 -> 0, of which waited for: 3 -> 0; matrix products, arithmetic and copies ran while one was open for 3% -> 0% of each run, Pallas kernels for 0% -> 0%
where the time goes in v1:
time: 161 us
  Pallas kernels  155 us (96%)
  local copies, waits for them, and re-layouts  5.12 us (3%)
    pallas_call x1, Pallas kernels, body(): pl.pallas_call(kernel, out_shape=(jax.ShapeDtypeStruct((ROWS, COLS), BF16...  155 us
    unnamed x5, local copies, waits for them, and re-layouts  4.43 us

profile of v1, /device:TPU:1, one launch (start us, length us, event | category | flops | bytes accessed | tf_op | source)
XLA Modules:
  0.0 161.1 jit_solution(9207389051256271002)
XLA Ops:
  0.6 0.8 copy.8
  1.4 0.1 reshape.11
  1.5 0.6 pad.4.nbr
  2.1 155.3 %impute_and_sketch.1 = (bf16[2048,512]{1,0:T(8,128)(2,1)}, f32[16,512]{1,0:T(8,128)}) custom-call(bf16[2048,512]{1,0:T(8,128)(2,1)} %rat.1, s32[2048,512]{1,0:T(8,128)} %obs.1, bf16[4,384,512]{2,1,0:T(8,128)(2,1)} %bitcast.1, s32[8,128]{1,0:T(8,128)} %pad.4.nbr, bf16[2048,256]{1,0:T(8,128)(2,1)} %test.1), custom_call_target="tpu_custom_call" | custom-call | tf_op jit(solution)/shard_map/impute_and_sketch/pallas_call | solution.py:421
  157.4 0.0 copy-start
  157.4 3.0 %copy.11 = bf16[2048,512]{1,0:T(8,128)(2,1)} copy(bf16[2048,512]{1,0:T(8,128)(2,1)} %get-tuple-element.4) | data formatting | bytes 4194304
  160.4 0.0 copy-done
  160.4 0.6 copy.12
Async XLA Ops:
  157.4 3.1 %copy-start = (f32[16,512]{1,0:T(8,128)S(1)}, f32[16,512]{1,0:T(8,128)}, u32[]{:S(2)}) copy-start(f32[16,512]{1,0:T(8,128)} %get-tuple-element.5) | copy-start | bytes 98308

commit v2 on v1

--- a/solution.py
+++ b/solution.py
@@ -34,7 +34,7 @@
 PR = PBLK // SIDE
 PC = COLS // SIDE
 ITEMS = COLS * ITEM_DEVS
-LAG = 5
+LAG = 1
 
 ORDER = [
     (2, 2), (3, 2), (2, 3), (1, 2), (2, 1), (0, 2), (2, 0), (3, 1),
@@ -60,11 +60,11 @@
 def kernel(
     rat, obs, pool, nbr, test, imp, sketch,
     rat_v, obs_v, pool_v, test_v, nb_v, nb_s, spread, send2, near, cent, qm,
-    st_own, st_in, ms_own, ms_all, sib_out, sib_in, own,
-    up_out, up_in, dn_out, dn_in, wts, imp_v, sk, sk_in,
-    ld, nb_ss, nb_rs, s1_ss, s1_rs, s2_ss, s2_rs, st_ss, st_rs, ms_ss, ms_rs,
+    st_own, st_in, st_sib, st_qm, ms_own, ms_all, sib_out, sib_in, own,
+    up_out, up_in, dn_out, dn_in, wts, sk, sk_out, sk_in,
+    ld, nb_ss, nb_rs, s1_ss, s1_rs, s2_ss, s2_rs, su_ss, su_rs, sd_ss, sd_rs, sx_ss, sx_rs, ms_ss, ms_rs,
     sib_ss, sib_rs, up_ss, up_rs, dn_ss, dn_rs, au_ss, au_rs, ad_ss, ad_rs,
-    ax_ss, ax_rs, sk_ss, sk_rs, out_s,
+    ax_ss, ax_rs, sk_ss, sk_rs,
 ):
     u = lax.axis_index("users")
     it = lax.axis_index("items")
@@ -79,6 +79,7 @@
         return (u, ((z + dz + CHIPS) % CHIPS) * 2 + c)
 
     sibling = (u, z * 2 + (1 - c))
+    up, down = chip_at(1), chip_at(-1)
 
     def send(src, dst, ss, rs, dev):
         copy = pltpu.make_async_remote_copy(
@@ -115,11 +116,9 @@
     barrier = pltpu.get_barrier_semaphore()
     for dx, dy in ORDER:
         pl.semaphore_signal(barrier, inc=1, device_id=(user_at(dx, dy), it), device_id_type=MESH)
-    for k in range(1, ITEM_DEVS):
-        pl.semaphore_signal(
-            barrier, inc=1, device_id=(u, (it + k) % ITEM_DEVS), device_id_type=MESH
-        )
-    pl.semaphore_wait(barrier, USERS - 1 + ITEM_DEVS - 1)
+    for neighbour in (sibling, up, down):
+        pl.semaphore_signal(barrier, inc=1, device_id=neighbour, device_id_type=MESH)
+    pl.semaphore_wait(barrier, USERS - 1 + 3)
 
     for o, (dx, dy) in enumerate(ORDER):
         t = user_at(dx, dy)
@@ -150,12 +149,34 @@
         masked = (seen * rat_v[rows].astype(F32)).astype(BF16)
         st_own[0:1, rows] = nt(ones, masked)[0:1]
         st_own[1:2, rows] = nt(ones, seen.astype(BF16))[0:1]
-    for k in range(1, ITEM_DEVS):
-        send(
-            st_own, st_in.at[it], st_ss.at[k - 1], st_rs.at[k - 1],
-            (u, (it + k) % ITEM_DEVS),
-        )
-    st_in[it] = st_own[...]
+    st_in[z] = st_own[...]
+
+    def stats_from(d):
+        return st_in.at[(z + d + CHIPS) % CHIPS]
+
+    for s in range(PLUS):
+        if s > 0:
+            arrived(stats_from(-s), su_ss.at[s - 1], su_rs.at[s - 1])
+        send(stats_from(-s), stats_from(-s), su_ss.at[s], su_rs.at[s], up)
+        if s < MINUS:
+            if s > 0:
+                arrived(stats_from(s), sd_ss.at[s - 1], sd_rs.at[s - 1])
+            send(stats_from(s), stats_from(s), sd_ss.at[s], sd_rs.at[s], down)
+    arrived(stats_from(-PLUS), su_ss.at[PLUS - 1], su_rs.at[PLUS - 1])
+    arrived(stats_from(MINUS), sd_ss.at[MINUS - 1], sd_rs.at[MINUS - 1])
+
+    sums = st_in[0]
+    for k in range(1, CHIPS):
+        sums = sums + st_in[k]
+    core_mean = sums[2:3, 0:PROWS] * (1.0 / (CHIPS * COLS))
+    squares = sums[3:4, 0:PROWS]
+    for k in range(CHIPS):
+        gap = st_in[k, 2:3, 0:PROWS] * (1.0 / COLS) - core_mean
+        squares = squares + COLS * (gap * gap)
+    st_own[0:2] = sums[0:2]
+    st_own[2:3, 0:PROWS] = core_mean
+    st_own[3:4, 0:PROWS] = squares
+    send(st_own, st_sib, sx_ss.at[0], sx_rs.at[0], sibling)
 
     loads[4].wait()
     for o, (dx, dy) in enumerate(ORDER):
@@ -172,7 +193,7 @@
         for o, (dx, dy) in enumerate(ORDER):
             t = user_at(dx, dy)
             for k in range(b * NB, (b + 1) * NB):
-                send2[o, k] = spread[nb_s[t, 0, k]]
+                send2[o, k] = spread[nb_s[t, k // NB, k % NB]]
             send(
                 send2.at[o, pl.ds(b * NB, NB)],
                 near.at[pl.ds(b * NB, NB), pl.ds(ux * PR, PR), pl.ds(pl.multiple_of(uy * PC, PC), PC)],
@@ -180,7 +201,7 @@
             )
         for k in range(b * NB, (b + 1) * NB):
             near[k, pl.ds(pl.multiple_of(ux * PR, PR), PR), pl.ds(pl.multiple_of(uy * PC, PC), PC)] = spread[
-                nb_s[u, 0, k]
+                nb_s[u, k // NB, k % NB]
             ]
 
     def delivered(b):
@@ -198,17 +219,11 @@
     deliver(0)
     deliver(1)
 
-    for k in range(1, ITEM_DEVS):
-        src = (it + ITEM_DEVS - k) % ITEM_DEVS
-        arrived(st_in.at[src], st_ss.at[k - 1], st_rs.at[k - 1])
-    sums = st_in[0]
-    for k in range(1, ITEM_DEVS):
-        sums = sums + st_in[k]
-    pool_mean = sums[2:3, 0:PROWS] * (1.0 / ITEMS)
-    squares = sums[3:4, 0:PROWS]
-    for k in range(ITEM_DEVS):
-        gap = st_in[k, 2:3, 0:PROWS] * (1.0 / COLS) - pool_mean
-        squares = squares + COLS * (gap * gap)
+    arrived(st_sib, sx_ss.at[0], sx_rs.at[0])
+    core_mean, other_mean = st_own[2:3, 0:PROWS], st_sib[2:3, 0:PROWS]
+    pool_mean = (core_mean + other_mean) * 0.5
+    gap = core_mean - other_mean
+    squares = (st_own[3:4, 0:PROWS] + st_sib[3:4, 0:PROWS]) + (CHIPS * COLS * 0.5) * (gap * gap)
     scale = lax.rsqrt(squares * (1.0 / ITEMS) + 1e-05)
     blank = jnp.zeros((2, 128), F32)
     for b in range(PB):
@@ -228,7 +243,7 @@
 
     def spread_mean(k, carry):
         at = pl.multiple_of(k * 128, 128)
-        row = st_own[0:1, pl.ds(at, 128)]
+        row = st_qm[0:1, pl.ds(at, 128)]
         wide = jnp.broadcast_to(row, (128, 128)).T
         qm[pl.ds(at, 128)] = wide
         mean = jnp.concatenate([wide] * (COLS // 128), axis=1)
@@ -236,23 +251,19 @@
         cent[pl.ds(at, 128)] = (seen * (rat_v[pl.ds(at, 128)].astype(F32) - mean)).astype(BF16)
         return carry
 
-    for copy in sent[2 * (USERS - 1):2 * (USERS - 1) + ITEM_DEVS - 1]:
-        copy.wait_send()
-    del sent[2 * (USERS - 1):2 * (USERS - 1) + ITEM_DEVS - 1]
-    st_own[0:1] = sums[0:1] / (sums[1:2] + 1.0)
+    st_qm[...] = (st_own[0:1] + st_sib[0:1]) / (st_own[1:2] + st_sib[1:2] + 1.0)
     lax.fori_loop(0, ROWS // 128, spread_mean, 0)
     for o, (dx, dy) in enumerate(ORDER):
         src = user_at(-dx + SIDE, -dy + SIDE)
         arrived(ms_all.at[pl.ds(src * (PB // 2), PB // 2)], ms_ss.at[o], ms_rs.at[o])
     loads[3].wait()
 
-    up, down = chip_at(1), chip_at(-1)
     mine_at = c * HALF
 
     def stats_of(b):
         means, scales = [], []
         for k in range(b * NB, (b + 1) * NB):
-            n = nb_s[u, 0, k]
+            n = nb_s[u, k // NB, k % NB]
             pair = ms_all[n // 2].astype(F32)
             tile = jnp.where(n % 2 == 0, pair[0:8], pair[8:16])
             means += [tile[j:j + 1] for j in range(3)]
@@ -268,7 +279,7 @@
         rows = pl.ds(b * QBLK + at, HALF)
         base = qm[rows] - nt(w, mean_mat)
         filled = jnp.concatenate([base] * (COLS // 128), axis=1) + shift
-        imp_v[rows] = jnp.where(obs_v[rows] > 0, rat_v[rows].astype(F32), filled).astype(BF16)
+        imp[rows] = jnp.where(obs_v[rows] > 0, rat_v[rows].astype(F32), filled).astype(BF16)
 
     def block(b):
         yield
@@ -344,9 +355,8 @@
             arrived(place(-s, 1 - c), ax_ss.at[b, MINUS + s], ax_rs.at[b, MINUS + s])
         fill(b, pl.multiple_of((1 - c) * HALF, HALF))
         rows = slice(b * QBLK, (b + 1) * QBLK)
-        pltpu.make_async_copy(imp_v.at[rows], imp.at[rows], out_s.at[b]).start()
         part = lax.dot_general(
-            test_v[rows], imp_v[rows], (((0,), (0,)), ((), ())), preferred_element_type=F32
+            test_v[rows], imp[rows], (((0,), (0,)), ((), ())), preferred_element_type=F32
         ).reshape(USERS, KS // USERS, COLS)
         sk[...] = part if b == 0 else sk[...] + part
 
@@ -359,27 +369,23 @@
                 live.remove(b)
         tick += 1
 
+    sk_out[...] = sk[...].astype(BF16)
     for o, (dx, dy) in enumerate(ORDER):
         t = user_at(dx, dy)
-        send(sk.at[t], sk_in.at[u], sk_ss.at[o], sk_rs.at[o], (t, it))
-    sk_in[u] = sk[u]
+        send(sk_out.at[t], sk_in.at[u], sk_ss.at[o], sk_rs.at[o], (t, it))
     for copy in sent[:-(USERS - 1)]:
         copy.wait_send()
     del sent[:-(USERS - 1)]
-    for b in range(QB):
-        rows = slice(b * QBLK, (b + 1) * QBLK)
-        pltpu.make_async_copy(imp_v.at[rows], imp.at[rows], out_s.at[b]).wait()
     for o, (dx, dy) in enumerate(ORDER):
         arrived(sk_in.at[user_at(-dx + SIDE, -dy + SIDE)], sk_ss.at[o], sk_rs.at[o])
-    total = sk_in[0]
-    for k in range(1, USERS):
-        total = total + sk_in[k]
+    total = sk[u]
+    for dx, dy in ORDER:
+        total = total + sk_in[user_at(dx, dy)].astype(F32)
     sketch[...] = total * (1.0 / math.sqrt(ROWS * USERS))
     flush()
 
 
 def body(ratings, observed, pool_profiles, neighbours, test_matrix):
-    lists = jnp.pad(neighbours.reshape(1, REQ), ((0, 7), (0, 128 - REQ)))
     pool = pool_profiles.reshape(PB, PBLK, COLS)
     dma = pltpu.SemaphoreType.DMA
     n = USERS - 1
@@ -388,15 +394,17 @@
         pltpu.VMEM((ROWS, COLS), jnp.int32),
         pltpu.VMEM((PB, PBLK, COLS), BF16),
         pltpu.VMEM((ROWS, KS), BF16),
-        pltpu.VMEM((USERS, 8, 128), jnp.int32),
-        pltpu.SMEM((USERS, 8, 128), jnp.int32),
+        pltpu.VMEM((USERS, QB, NB), jnp.int32),
+        pltpu.SMEM((USERS, QB, NB), jnp.int32),
         pltpu.VMEM((USERS * PB, PR, PC), BF16),
         pltpu.VMEM((n, REQ, PR, PC), BF16),
         pltpu.VMEM((REQ, PBLK, COLS), BF16),
         pltpu.VMEM((ROWS, COLS), BF16),
         pltpu.VMEM((ROWS, 128), F32),
         pltpu.VMEM((4, ROWS), F32),
-        pltpu.VMEM((ITEM_DEVS, 4, ROWS), F32),
+        pltpu.VMEM((CHIPS, 4, ROWS), F32),
+        pltpu.VMEM((4, ROWS), F32),
+        pltpu.VMEM((1, ROWS), F32),
         pltpu.VMEM((PB // 2, 16, 128), F32),
         pltpu.VMEM((USERS * PB // 2, 16, 128), BF16),
         pltpu.VMEM((QB, HALF, NEAR), BF16),
@@ -407,31 +415,30 @@
         pltpu.VMEM((QB, MINUS, CHUNK, NEAR), BF16),
         pltpu.VMEM((QB, MINUS, CHUNK, NEAR), BF16),
         pltpu.VMEM((QB, QBLK, NEAR), BF16),
-        pltpu.VMEM((ROWS, COLS), BF16),
         pltpu.VMEM((USERS, KS // USERS, COLS), F32),
-        pltpu.VMEM((USERS, KS // USERS, COLS), F32),
+        pltpu.VMEM((USERS, KS // USERS, COLS), BF16),
+        pltpu.VMEM((USERS, KS // USERS, COLS), BF16),
         dma((7,)),
     ]
-    for shape in ((n,), (n,), (QB, n), (ITEM_DEVS - 1,), (n,), (QB,), (QB, PLUS), (QB, MINUS),
+    for shape in ((n,), (n,), (QB, n), (PLUS,), (MINUS,), (1,), (n,), (QB,), (QB, PLUS), (QB, MINUS),
                   (QB, PLUS), (QB, MINUS), (QB, CHIPS), (n,)):
         scratch += [dma(shape), dma(shape)]
-    scratch.append(dma((QB,)))
     hbm = pl.BlockSpec(memory_space=pl.ANY)
     vmem = pl.BlockSpec(memory_space=pltpu.VMEM)
     return pl.pallas_call(
         kernel,
         out_shape=(
-            jax.ShapeDtypeStruct((ROWS, COLS), BF16),
-            jax.ShapeDtypeStruct((KS // USERS, COLS), F32),
+            pltpu.VMEM((ROWS, COLS), BF16),
+            pltpu.VMEM((KS // USERS, COLS), F32),
         ),
         in_specs=[hbm, hbm, hbm, vmem, hbm],
-        out_specs=(hbm, vmem),
+        out_specs=(vmem, vmem),
         scratch_shapes=scratch,
         compiler_params=pltpu.CompilerParams(
-            collective_id=0, has_side_effects=True, vmem_limit_bytes=56 * 2**20
+            collective_id=0, has_side_effects=True, vmem_limit_bytes=58 * 2**20
         ),
         name="impute_and_sketch",
-    )(ratings, observed, pool, lists, test_matrix)
+    )(ratings, observed, pool, neighbours, test_matrix)
 
 
 def solution(mesh):

time: 161 us -> 120 us (0.75)
  Pallas kernels: 155 us -> 116 us
  local copies, waits for them, and re-layouts: 5.12 us -> 3.27 us
    pallas_call x1, Pallas kernels: 155 us -> 116 us  [body(): pl.pallas_call(kernel, out_shape=(pltpu.VMEM((ROWS, COLS), BF16), pltpu.V...]
    unnamed x5 -> x3, local copies, waits for them, and re-layouts: 4.43 us -> 3.27 us
where the time goes in v2:
time: 120 us
  Pallas kernels  116 us (97%)
  local copies, waits for them, and re-layouts  3.27 us (3%)
    pallas_call x1, Pallas kernels, body(): pl.pallas_call(kernel, out_shape=(pltpu.VMEM((ROWS, COLS), BF16), pltpu.V...  116 us
    unnamed x3, local copies, waits for them, and re-layouts  3.27 us

profile of v2, /device:TPU:1, one launch (start us, length us, event | category | flops | bytes accessed | tf_op | source)
XLA Modules:
  0.0 119.9 jit_solution(4271305378148191964)
XLA Ops:
  0.6 1.3 %copy.7.nbr = s32[4,2]{1,0:T(4,128)} copy(s32[4,2]{0,1:T(2,128)} %param.8) | data formatting | bytes 64 | tf_op args[3]
  2.0 116.0 %impute_and_sketch.1 = (bf16[2048,512]{1,0:T(8,128)(2,1)S(1)}, f32[16,512]{1,0:T(8,128)S(1)}) custom-call(bf16[2048,512]{1,0:T(8,128)(2,1)} %rat.1, s32[2048,512]{1,0:T(8,128)} %obs.1, bf16[4,384,512]{2,1,0:T(8,128)(2,1)} %bitcast.1, s32[4,2]{1,0:T(4,128)} %copy.7.nbr, bf16[2048,256]{1,0:T(8,128)(2,1)} %test.1), custom_call_target="tpu_custom_call" | custom-call | tf_op jit(solution)/shard_map/impute_and_sketch/pallas_call | solution.py:428
  117.9 1.3 %copy.10 = bf16[2048,512]{1,0:T(8,128)(2,1)} copy(bf16[2048,512]{1,0:T(8,128)(2,1)S(1)} %get-tuple-element.2) | data formatting | bytes 4194304
  119.2 0.6 copy.11

commit v3 on v2

--- a/solution.py
+++ b/solution.py
@@ -37,8 +37,8 @@
 LAG = 1
 
 ORDER = [
-    (2, 2), (3, 2), (2, 3), (1, 2), (2, 1), (0, 2), (2, 0), (3, 1),
-    (1, 3), (3, 3), (1, 1), (0, 3), (3, 0), (0, 1), (1, 0),
+    (2, 2), (1, 0), (0, 1), (2, 1), (0, 3), (3, 0), (1, 2), (2, 3),
+    (3, 2), (1, 1), (3, 3), (2, 0), (0, 2), (1, 3), (3, 1),
 ]
 
 
@@ -193,7 +193,7 @@
         for o, (dx, dy) in enumerate(ORDER):
             t = user_at(dx, dy)
             for k in range(b * NB, (b + 1) * NB):
-                send2[o, k] = spread[nb_s[t, k // NB, k % NB]]
+                send2[o, k] = spread[nb_s[t, k % NB, k // NB]]
             send(
                 send2.at[o, pl.ds(b * NB, NB)],
                 near.at[pl.ds(b * NB, NB), pl.ds(ux * PR, PR), pl.ds(pl.multiple_of(uy * PC, PC), PC)],
@@ -201,7 +201,7 @@
             )
         for k in range(b * NB, (b + 1) * NB):
             near[k, pl.ds(pl.multiple_of(ux * PR, PR), PR), pl.ds(pl.multiple_of(uy * PC, PC), PC)] = spread[
-                nb_s[u, k // NB, k % NB]
+                nb_s[u, k % NB, k // NB]
             ]
 
     def delivered(b):
@@ -263,7 +263,7 @@
     def stats_of(b):
         means, scales = [], []
         for k in range(b * NB, (b + 1) * NB):
-            n = nb_s[u, k // NB, k % NB]
+            n = nb_s[u, k % NB, k // NB]
             pair = ms_all[n // 2].astype(F32)
             tile = jnp.where(n % 2 == 0, pair[0:8], pair[8:16])
             means += [tile[j:j + 1] for j in range(3)]
@@ -394,8 +394,8 @@
         pltpu.VMEM((ROWS, COLS), jnp.int32),
         pltpu.VMEM((PB, PBLK, COLS), BF16),
         pltpu.VMEM((ROWS, KS), BF16),
-        pltpu.VMEM((USERS, QB, NB), jnp.int32),
-        pltpu.SMEM((USERS, QB, NB), jnp.int32),
+        pltpu.VMEM((USERS, NB, QB), jnp.int32),
+        pltpu.SMEM((USERS, NB, QB), jnp.int32),
         pltpu.VMEM((USERS * PB, PR, PC), BF16),
         pltpu.VMEM((n, REQ, PR, PC), BF16),
         pltpu.VMEM((REQ, PBLK, COLS), BF16),
@@ -431,14 +431,14 @@
             pltpu.VMEM((ROWS, COLS), BF16),
             pltpu.VMEM((KS // USERS, COLS), F32),
         ),
-        in_specs=[hbm, hbm, hbm, vmem, hbm],
+        in_specs=[hbm, hbm, hbm, hbm, hbm],
         out_specs=(vmem, vmem),
         scratch_shapes=scratch,
         compiler_params=pltpu.CompilerParams(
             collective_id=0, has_side_effects=True, vmem_limit_bytes=58 * 2**20
         ),
         name="impute_and_sketch",
-    )(ratings, observed, pool, neighbours, test_matrix)
+    )(ratings, observed, pool, neighbours.T, test_matrix)
 
 
 def solution(mesh):

time: 120 us -> 118 us (0.983)
  local copies, waits for them, and re-layouts: 3.27 us -> 1.94 us
    unnamed x3 -> x2, local copies, waits for them, and re-layouts: 3.27 us -> 1.94 us
where the time goes in v3:
time: 118 us
  Pallas kernels  116 us (98%)
  local copies, waits for them, and re-layouts  1.94 us (2%)
    pallas_call x1, Pallas kernels, body(): pl.pallas_call(kernel, out_shape=(pltpu.VMEM((ROWS, COLS), BF16), pltpu.V...  116 us

profile of v3, /device:TPU:1, one launch (start us, length us, event | category | flops | bytes accessed | tf_op | source)
XLA Modules:
  0.0 118.3 jit_solution(16929531416482408127)
XLA Ops:
  0.6 115.7 %impute_and_sketch.1 = (bf16[2048,512]{1,0:T(8,128)(2,1)S(1)}, f32[16,512]{1,0:T(8,128)S(1)}) custom-call(bf16[2048,512]{1,0:T(8,128)(2,1)} %rat.1, s32[2048,512]{1,0:T(8,128)} %obs.1, bf16[4,384,512]{2,1,0:T(8,128)(2,1)} %bitcast.2, s32[2,4]{1,0:T(2,128)} %bitcast.3, bf16[2048,256]{1,0:T(8,128)(2,1)} %test.1), custom_call_target="tpu_custom_call" | custom-call | tf_op jit(solution)/shard_map/impute_and_sketch/pallas_call | solution.py:428
  116.3 1.3 %copy.9 = bf16[2048,512]{1,0:T(8,128)(2,1)} copy(bf16[2048,512]{1,0:T(8,128)(2,1)S(1)} %get-tuple-element.2) | data formatting | bytes 4194304
  117.7 0.6 copy.10

commit v4 on v3

--- a/solution.py
+++ b/solution.py
@@ -178,47 +178,6 @@
     st_own[3:4, 0:PROWS] = squares
     send(st_own, st_sib, sx_ss.at[0], sx_rs.at[0], sibling)
 
-    loads[4].wait()
-    for o, (dx, dy) in enumerate(ORDER):
-        arrived(nb_v.at[user_at(-dx + SIDE, -dy + SIDE)], nb_ss.at[o], nb_rs.at[o])
-    lists = pltpu.make_async_copy(nb_v, nb_s, ld.at[6])
-    lists.start()
-    lists.wait()
-    loads[5].wait()
-    for o, (dx, dy) in enumerate(ORDER):
-        src = user_at(-dx + SIDE, -dy + SIDE)
-        arrived(spread.at[pl.ds(src * PB, PB)], s1_ss.at[o], s1_rs.at[o])
-
-    def deliver(b):
-        for o, (dx, dy) in enumerate(ORDER):
-            t = user_at(dx, dy)
-            for k in range(b * NB, (b + 1) * NB):
-                send2[o, k] = spread[nb_s[t, k % NB, k // NB]]
-            send(
-                send2.at[o, pl.ds(b * NB, NB)],
-                near.at[pl.ds(b * NB, NB), pl.ds(ux * PR, PR), pl.ds(pl.multiple_of(uy * PC, PC), PC)],
-                s2_ss.at[b, o], s2_rs.at[b, o], (t, it),
-            )
-        for k in range(b * NB, (b + 1) * NB):
-            near[k, pl.ds(pl.multiple_of(ux * PR, PR), PR), pl.ds(pl.multiple_of(uy * PC, PC), PC)] = spread[
-                nb_s[u, k % NB, k // NB]
-            ]
-
-    def delivered(b):
-        for o, (dx, dy) in enumerate(ORDER):
-            src = user_at(-dx + SIDE, -dy + SIDE)
-            arrived(
-                near.at[
-                    pl.ds(b * NB, NB),
-                    pl.ds((src // SIDE) * PR, PR),
-                    pl.ds(pl.multiple_of((src % SIDE) * PC, PC), PC),
-                ],
-                s2_ss.at[b, o], s2_rs.at[b, o],
-            )
-
-    deliver(0)
-    deliver(1)
-
     arrived(st_sib, sx_ss.at[0], sx_rs.at[0])
     core_mean, other_mean = st_own[2:3, 0:PROWS], st_sib[2:3, 0:PROWS]
     pool_mean = (core_mean + other_mean) * 0.5
@@ -238,6 +197,47 @@
     for o, (dx, dy) in enumerate(ORDER):
         mine = ms_all.at[pl.ds(u * (PB // 2), PB // 2)]
         send(mine, mine, ms_ss.at[o], ms_rs.at[o], (user_at(dx, dy), it))
+    loads[4].wait()
+    for o, (dx, dy) in enumerate(ORDER):
+        arrived(nb_v.at[user_at(-dx + SIDE, -dy + SIDE)], nb_ss.at[o], nb_rs.at[o])
+    lists = pltpu.make_async_copy(nb_v, nb_s, ld.at[6])
+    lists.start()
+    lists.wait()
+    loads[5].wait()
+    for o, (dx, dy) in enumerate(ORDER):
+        src = user_at(-dx + SIDE, -dy + SIDE)
+        arrived(spread.at[pl.ds(src * PB, PB)], s1_ss.at[o], s1_rs.at[o])
+
+    def deliver(b):
+        for o, (dx, dy) in enumerate(ORDER):
+            t = user_at(dx, dy)
+            for k in range(b * NB, (b + 1) * NB):
+                send2[o, k] = spread[nb_s[t, k % NB, k // NB]]
+            send(
+                send2.at[o, pl.ds(b * NB, NB)],
+                near.at[pl.ds(b * NB, NB), pl.ds(ux * PR, PR), pl.ds(pl.multiple_of(uy * PC, PC), PC)],
+                s2_ss.at[b, o], s2_rs.at[b, o], (t, it),
+            )
+        for k in range(b * NB, (b + 1) * NB):
+            near[k, pl.ds(pl.multiple_of(ux * PR, PR), PR), pl.ds(pl.multiple_of(uy * PC, PC), PC)] = spread[
+                nb_s[u, k % NB, k // NB]
+            ]
+
+    def delivered(b):
+        for o, (dx, dy) in enumerate(ORDER):
+            src = user_at(-dx + SIDE, -dy + SIDE)
+            arrived(
+                near.at[
+                    pl.ds(b * NB, NB),
+                    pl.ds((src // SIDE) * PR, PR),
+                    pl.ds(pl.multiple_of((src % SIDE) * PC, PC), PC),
+                ],
+                s2_ss.at[b, o], s2_rs.at[b, o],
+            )
+
+    deliver(0)
+    deliver(1)
+
     deliver(2)
     deliver(3)
 

time: 118 us -> 118 us (level)
  no operation moved by 1% of the time
where the time goes in v4:
time: 118 us
  Pallas kernels  115 us (97%)
  local copies, waits for them, and re-layouts  1.94 us (2%)
    pallas_call x1, Pallas kernels, body(): pl.pallas_call(kernel, out_shape=(pltpu.VMEM((ROWS, COLS), BF16), pltpu.V...  115 us

profile of v4, /device:TPU:1, one launch (start us, length us, event | category | flops | bytes accessed | tf_op | source)
XLA Modules:
  0.0 117.6 jit_solution(10417674810563793200)
XLA Ops:
  0.6 115.0 %impute_and_sketch.1 = (bf16[2048,512]{1,0:T(8,128)(2,1)S(1)}, f32[16,512]{1,0:T(8,128)S(1)}) custom-call(bf16[2048,512]{1,0:T(8,128)(2,1)} %rat.1, s32[2048,512]{1,0:T(8,128)} %obs.1, bf16[4,384,512]{2,1,0:T(8,128)(2,1)} %bitcast.2, s32[2,4]{1,0:T(2,128)} %bitcast.3, bf16[2048,256]{1,0:T(8,128)(2,1)} %test.1), custom_call_target="tpu_custom_call" | custom-call | tf_op jit(solution)/shard_map/impute_and_sketch/pallas_call | solution.py:428
  115.6 1.3 %copy.9 = bf16[2048,512]{1,0:T(8,128)(2,1)} copy(bf16[2048,512]{1,0:T(8,128)(2,1)S(1)} %get-tuple-element.2) | data formatting | bytes 4194304
  117.0 0.6 copy.10
